TPU v7x, 32 devices: a whole 2x2x4 slice. The times are simulated.
32 devices in a mesh: groups: 2 (over y), region: 4 (over z), strip: 2 (over x), chan: 2 (over core).
Axes of the slice: x: 2, y: 2, z: 4, core: 2. Of those that a mesh axis runs over, the one named last changes fastest.
Arguments:
- features: bfloat16 [128, 32, 512], P(('groups', 'region', 'strip'), 'chan'), parts along dimension 0, may hold values from -6 to 6
- out_grad: bfloat16 [128, 32, 512], P(('groups', 'region', 'strip'), 'chan'), parts along dimension 0, may hold values from -6 to 6
- weight: bfloat16 [27, 32, 32], P(None, 'chan'), may hold values from -0.21875 to 0.21875
- occupancy: int32 [128, 512], P(('groups', 'region', 'strip')), parts along dimension 0, may hold values from 0 to 1, as said below
- neighbours: int32 [128, 27], P(('groups', 'region', 'strip')), parts along dimension 0, may hold values from -1 to 63, as said below
Outputs:
- grad_features: bfloat16 [128, 32, 512], P(('groups', 'region', 'strip'), 'chan'), parts along dimension 0
- grad_weight: float32 [54, 32, 32], P('groups', 'chan'), parts along dimension 0
There are 2 independent parts, one for each index of `groups`. A program takes and returns all parts, laid end to end along the dimension named above; an argument that names none is the same for every part. Nothing has to cross between parts.
Inputs may be any that keep to these rules, and one draw needn't show every extreme that they name: `occupancy`: each brick has a level of 0 to 4, and each of its 512 voxels is occupied with probability level/4, independently; so some bricks are empty and some full. `neighbours`: the slots of a scene fill a box of 8 by 4 by 2 brick positions, one slot each, and entry t of a slot names the slot at its position moved by offset_t, or -1 outside the box. Slot s has brick coordinate s // 8 along the first dimension; index d of region+strip holds slots d * 8 to (d + 1) * 8 - 1. Entry 13 names the brick itself.
All inputs are finite; a program needn't handle non-finite values.
Results may differ from a plain program's by a relative error of at most 0.001.
Values may be sent and summed in bfloat16 or wider, within the bound.
A program may use at most 64 MiB of HBM per device.

v0:
```python
import math

import jax
import jax.numpy as jnp
from jax import lax
from jax.sharding import PartitionSpec as P

GY = 4
GZ = 2


def from_behind(block, axis, distance):
    devices = range(lax.axis_size(axis))
    route = [(i - distance, i) for i in devices if i - distance in devices]
    return lax.ppermute(block, axis, route)


def locate(global_ids, base_slot, slot_count, lower_count, upper_count):
    valid = global_ids >= 0
    relative = global_ids - base_slot
    inside = valid & (relative >= 0) & (relative < slot_count)
    before = valid & (relative < 0) & (relative >= -lower_count)
    after = valid & (relative >= slot_count) & (relative < slot_count + upper_count)
    empty_row = slot_count + lower_count + upper_count
    return jnp.where(
        inside,
        relative,
        jnp.where(
            before,
            slot_count + lower_count + relative,
            jnp.where(after, lower_count + relative, empty_row),
        ),
    )


def with_zero(array):
    return jnp.concatenate([array, jnp.zeros((1,) + array.shape[1:], array.dtype)], axis=0)


def shift_with(values_in, source, row_index, offset_step, stride, coord):
    own_part = jnp.roll(values_in, -offset_step * stride, axis=2)
    other_part = jnp.roll(jnp.take(source, row_index, axis=0), 7 * offset_step * stride, axis=2)
    edge_value = 7 if offset_step > 0 else 0
    return jnp.where((coord == edge_value)[None, None, :], other_part, own_part)


def local(features, out_grad, weight, occupancy, neighbours):
    slot_count = features.shape[0]
    face_count = GY * GZ
    device_count = lax.axis_size(("region", "strip"))
    base_slot = lax.axis_index(("region", "strip")) * slot_count
    occupied = occupancy.astype(jnp.bfloat16)
    masked_x = features * occupied[:, None, :]
    masked_part = out_grad * occupied[:, None, :]
    masked_g = lax.all_gather(masked_part, "chan", axis=1, tiled=True)
    lane_ids = jnp.arange(512, dtype=jnp.int32)
    coord_x = lane_ids // 64
    coord_y = lane_ids // 8 % 8
    coord_z = lane_ids % 8
    lower_x, lower_g = from_behind((masked_x, masked_g), ("region", "strip"), 1)
    upper_x, upper_g = from_behind((masked_x, masked_g), ("region", "strip"), -1)

    def across(values_in, lower_rows, upper_rows, offset_step):
        tap_index = 13 + 9 * offset_step
        row_index = locate(neighbours[:, tap_index], base_slot, slot_count, face_count, face_count)
        source = with_zero(jnp.concatenate([values_in, lower_rows, upper_rows], axis=0))
        return shift_with(values_in, source, row_index, offset_step, 64, coord_x)

    def inside(values_in, offset_step, stride, coord):
        tap_index = 13 + offset_step * (3 if stride == 8 else 1)
        row_index = locate(neighbours[:, tap_index], base_slot, slot_count, 0, 0)
        return shift_with(values_in, with_zero(values_in), row_index, offset_step, stride, coord)

    across_feats = [
        across(masked_x, lower_x, upper_x, -1),
        masked_x,
        across(masked_x, lower_x, upper_x, 1),
    ]
    across_grads = jnp.stack(
        [across(masked_g, lower_g, upper_g, 1), masked_g, across(masked_g, lower_g, upper_g, -1)]
    )
    depth_grads = [inside(masked_g, 1, 1, coord_z), masked_g, inside(masked_g, -1, 1, coord_z)]
    cross_list = []
    for index_y in range(3):
        for index_z in range(3):
            if index_y == 1:
                cross_list.append(depth_grads[index_z])
            else:
                cross_list.append(inside(depth_grads[index_z], 1 - index_y, 8, coord_y))
    cross_grads = jnp.stack(cross_list)
    term_list = [
        jnp.einsum(
            "bip,sbop->sio", across_feats[index_x], cross_grads, preferred_element_type=jnp.float32
        )
        for index_x in range(3)
    ]
    weight_terms = jnp.concatenate(term_list, axis=0)
    depth_sums = []
    for index_z in range(3):
        row_total = None
        for index_y in range(3):
            tap_weights = weight[3 * index_y + index_z :: 9]
            partial_rows = jnp.einsum(
                "xio,xbop->bip", tap_weights, across_grads, preferred_element_type=jnp.float32
            )
            if index_y != 1:
                partial_rows = inside(partial_rows, 1 - index_y, 8, coord_y)
            row_total = partial_rows if row_total is None else row_total + partial_rows
        depth_sums.append(row_total)
    grad_rows = (
        depth_sums[1] + inside(depth_sums[0], 1, 1, coord_z) + inside(depth_sums[2], -1, 1, coord_z)
    )
    grad_features = (grad_rows * occupancy.astype(jnp.float32)[:, None, :]).astype(jnp.bfloat16)
    scale_factor = 1.0 / math.sqrt(slot_count * device_count * 512)
    grad_weight = lax.psum(weight_terms, ("region", "strip")) * scale_factor
    return (grad_features, grad_weight)


def solution(mesh):
    placed = (
        P(("groups", "region", "strip"), "chan", None),
        P(("groups", "region", "strip"), "chan", None),
        P(None, "chan", None),
        P(("groups", "region", "strip"), None),
        P(("groups", "region", "strip"), None),
    )
    return jax.shard_map(
        local,
        mesh=mesh,
        in_specs=placed,
        out_specs=(P(("groups", "region", "strip"), "chan", None), P("groups", "chan", None)),
        check_vma=False,
    )
```

profile of v0, /device:TPU:0, one launch (start us, length us, event | category | flops | bytes accessed | tf_op | source)
XLA Modules:
  0.0 128.7 jit_solution(10644646143547188081)
XLA Ops:
  0.6 1.4 %fusion.70 = (f32[8,512]{1,0:T(8,128)}, bf16[8,512]{1,0:T(8,128)(2,1)S(1)}) fusion(s32[8,512]{1,0:T(8,128)} %param.16), kind=kLoop, calls=%fused_computation.252 | loop fusion | flops 8192 | bytes 40960 | tf_op jit(solution)/shard_map/convert_element_type | solution.py:113
  2.0 1.0 broadcast_multiply_fusion.1
  3.0 5.5 %collective-permute-start.2 = (bf16[8,16,512]{2,1,0:T(8,128)(2,1)S(1)}, bf16[8,16,512]{2,1,0:T(8,128)(2,1)}, u32[]{:S(2)}, u32[]{:S(2)}) collective-permute-start(bf16[8,16,512]{2,1,0:T(8,128)(2,1)S(1)} %get-tuple-element.68), channel_id=1, source_target_pairs={{0,2},{2,4},{4,6},{6,8},{8,10},{10,12},{12,14},{1,3},{3,5},{5,7},{... | collective-permute-start | bytes 393224 | tf_op jit(solution)/shard_map/ppermute | solution.py:15
  8.5 1.3 collective-permute-start.3
  9.8 2.0 %all_gather.3 = bf16[8,32,512]{2,1,0:T(8,128)(2,1)S(1)} all-gather(bf16[8,16,512]{2,1,0:T(8,128)(2,1)S(1)} %get-tuple-element.69), channel_id=1, replica_groups=mesh['groups'=2,'region'=4,'strip'=2,'chan'=2] {'chan'}, dimensions={1}, use_global_device_ids=true | all-gather | bytes 393216 | tf_op jit(solution)/shard_map/all_gather | solution.py:55
  11.8 5.2 %collective-permute-start = (bf16[8,32,512]{2,1,0:T(8,128)(2,1)S(1)}, bf16[8,32,512]{2,1,0:T(8,128)(2,1)}, u32[]{:S(2)}, u32[]{:S(2)}) collective-permute-start(bf16[8,32,512]{2,1,0:T(8,128)(2,1)S(1)} %all_gather.3), channel_id=1, source_target_pairs={{0,2},{2,4},{4,6},{6,8},{8,10},{10,12},{12,14},{1,3},{3,5},{5,7},{... | collective-permute-start | bytes 786440 | tf_op jit(solution)/shard_map/ppermute | solution.py:15
  17.1 1.3 collective-permute-start.1
  18.3 1.7 %compare_reduce_fusion = (pred[8]{0:T(512)(128)(4,1)S(1)}, pred[8]{0:T(512)(128)(4,1)S(1)}, pred[8]{0:T(512)(128)(4,1)S(1)}, pred[8]{0:T(512)(128)(4,1)}, pred[8]{0:T(512)(128)(4,1)}, /*index=5*/pred[8]{0:T(512)(128)(4,1)S(1)}) fusion(s32[8,27]{1,0:T(8,128)} %param.17), kind=kLoop, calls=%fused_computation.186 | loop fusion | flops 48 | bytes 240 | tf_op jit(solution)/shard_map/ge | solution.py:19
  20.1 1.7 %subtract_reduce_fusion = (s32[8]{0:T(128)S(1)}, s32[8]{0:T(128)}, s32[8]{0:T(128)}, s32[8]{0:T(128)S(1)}, s32[8]{0:T(128)S(1)}, /*index=5*/s32[8]{0:T(128)S(1)}) fusion(s32[8,27]{1,0:T(8,128)} %param.17, s32[]{:T(128)S(6)} %mul.37), kind=kLoop, calls=%fused_computation.173 | loop fusion | flops 48 | bytes 388 | tf_op jit(solution)/shard_map/sub | solution.py:20
  22.6 0.7 slice_bitcast_fusion.35
  23.4 0.9 slice_bitcast_fusion.36
  24.2 0.7 slice_bitcast_fusion.32
  25.9 0.7 slice_bitcast_fusion.33
  27.4 1.3 gather_fusion.11
  28.8 1.3 %gather_fusion.14 = bf16[8,32,512]{2,1,0:T(8,128)(2,1)} fusion(bf16[9,32,512]{2,1,0:T(8,128)(2,1)S(1)} %concatenate.476, s32[1024]{0:T(1024)S(1)} %pad_clamp_fusion.3), kind=kCustom, calls=%fused_computation.15.clone | custom fusion | bytes 524320 | tf_op jit(solution)/shard_map/jit(_take)/gather | solution.py:42
  30.1 1.2 broadcast_select_fusion.4
  31.4 0.7 slice_bitcast_fusion.27
  32.1 0.9 slice_bitcast_fusion.4
  33.0 0.7 slice_bitcast_fusion.20
  33.7 0.7 slice_bitcast_fusion.9
  34.4 0.7 slice_bitcast_fusion.25
  35.1 0.9 slice_bitcast_fusion.2
  36.0 0.7 slice_bitcast_fusion.18
  36.7 0.7 slice_bitcast_fusion.7
  37.5 0.7 slice_bitcast_fusion.23
  38.2 0.9 slice_bitcast_fusion
  39.1 0.7 slice_bitcast_fusion.16
  42.3 0.8 fusion.69
  43.0 0.7 fusion.68
  44.2 0.9 slice_bitcast_fusion.14
  45.1 0.7 slice_bitcast_fusion.30
  49.0 2.2 %convolution_bitcast_fusion.10 = f32[9,16,32]{2,1,0:T(8,128)} fusion(bf16[9,8,32,512]{3,2,1,0:T(8,128)(2,1)S(1)} %fusion.19, bf16[8,16,512]{2,1,0:T(8,128)(2,1)S(1)} %get-tuple-element.68), kind=kOutput, calls=%fused_computation.40 | convolution fusion | flops 37748736 | bytes 2508800 | tf_op jit(solution)/shard_map/bip,sbop->sio/dot_general | solution.py:92
  51.8 1.1 maximum_maximum_fusion.1
  53.7 0.6 slice.559
  54.3 0.7 gather_fusion.18
  55.0 0.8 broadcast_select_fusion.19
  56.0 2.3 %convolution_bitcast_fusion.11 = f32[9,16,32]{2,1,0:T(8,128)S(1)} fusion(bf16[9,8,32,512]{3,2,1,0:T(8,128)(2,1)S(1)} %fusion.19, bf16[8,16,448]{2,1,0:T(8,128)(2,1)S(1)} %bitcast.231, bf16[8,16,64]{2,1,0:T(8,128)(2,1)S(1)} %slice.554, bf16[8,16,448]{2,1,0:T(8,128)(2,1)S(1)} %copy-done.15, bf16[8,16,64]{2,1,0:T(8,128)(2,1)} %get-tuple-element.62, ...), kind=kOutput, calls=%fused_computation.41 | convolution fusion | flops 38338560 | bytes 2640384 | tf_op jit(solution)/shard_map/bip,sbop->sio/dot_general | solution.py:92
  58.4 1.5 %convolution_bitcast_fusion.9 = f32[9,16,32]{2,1,0:T(8,128)S(1)} fusion(bf16[9,8,32,512]{3,2,1,0:T(8,128)(2,1)S(1)} %fusion.19, bf16[8,16,64]{2,1,0:T(8,128)(2,1)S(1)} %copy-done.43, bf16[8,16,448]{2,1,0:T(8,128)(2,1)S(1)} %slice.558, bf16[8,16,64]{2,1,0:T(8,128)(2,1)S(1)} %copy-done.44, bf16[8,16,448]{2,1,0:T(8,128)(2,1)S(1)} %copy-done.14, ...), kind=kOutput, calls=%fused_computation.39 | convolution fusion | flops 38338560 | bytes 2640384 | tf_op jit(solution)/shard_map/bip,sbop->sio/dot_general | solution.py:92
  59.9 41.5 %psum.7 = f32[27,16,32]{2,1,0:T(8,128)S(1)} all-reduce(f32[27,16,32]{2,1,0:T(8,128)S(1)} %pad_maximum_fusion.1), channel_id=1, replica_groups=mesh['groups'=2,'region'=4,'strip'=2,'chan'=2] {'region','strip'}, use_global_device_ids=true, to_apply=%region_0.5 | all-reduce | flops 13824 | bytes 110592 | tf_op jit(solution)/shard_map/psum | solution.py:115
  101.5 0.7 broadcast_multiply_fusion
  102.2 1.2 maximum_maximum_fusion
  103.4 0.7 gather_fusion
  104.4 0.7 gather_fusion.1
  107.1 0.7 gather_fusion.3
  107.9 0.7 gather_fusion.5
  108.6 0.7 gather_fusion.8
  109.5 0.9 slice.514
  110.4 0.7 slice.516
  111.8 1.1 convolution_bitcast_fusion.2
  112.9 0.8 slice.512
  113.8 0.7 gather_fusion.2
  114.5 0.7 gather_fusion.4
  115.2 0.7 gather_fusion.7
  116.0 1.0 broadcast_select_fusion.12
  117.4 1.1 fusion.5
  118.5 0.8 gather_fusion.9
  120.4 1.1 fusion.4
  121.7 0.6 slice.509
  122.4 0.8 slice.494
  123.2 0.6 slice.495
  123.9 0.9 slice.492
  124.8 0.6 slice.493
  125.4 0.7 gather_fusion.6
  126.5 2.2 %fusion.9 = bf16[8,16,512]{2,1,0:T(8,128)(2,1)} fusion(f32[8,16,456]{2,1,0:T(8,128)S(1)} %bitcast.237, f32[8,16,56]{2,1,0:T(8,128)S(1)} %slice.490, f32[8,16,8]{2,1,0:T(8,128)} %slice.493, f32[8,16,504]{2,1,0:T(8,128)} %slice.492, f32[8,16,56]{2,1,0:T(8,128)S(1)} %copy-done.46, f32[8,16,456]{2,1,0:T(8,128)S(1)} %copy-done.30, ...), kind=kOutput, calls=%fused_computation.38 | convolution fusion | flops 16121856 | bytes 3110912 | tf_op jit(solution)/shard_map/xio,xbop->bip/dot_general | solution.py:103
  (261 shorter events, 15.0 us)
Async XLA Ops:
  3.0 48.8 %collective-permute-start.2 = (bf16[8,16,512]{2,1,0:T(8,128)(2,1)S(1)}, bf16[8,16,512]{2,1,0:T(8,128)(2,1)}, u32[]{:S(2)}, u32[]{:S(2)}) collective-permute-start(bf16[8,16,512]{2,1,0:T(8,128)(2,1)S(1)} %get-tuple-element.68), channel_id=1, source_target_pairs={{0,2},{2,4},{4,6},{6,8},{8,10},{10,12},{12,14},{1,3},{3,5},{5,7},{... | collective-permute-start | bytes 393224 | tf_op jit(solution)/shard_map/ppermute | solution.py:15
  8.5 43.3 %collective-permute-start.3 = (bf16[8,16,512]{2,1,0:T(8,128)(2,1)S(1)}, bf16[8,16,512]{2,1,0:T(8,128)(2,1)}, u32[]{:S(2)}, u32[]{:S(2)}) collective-permute-start(bf16[8,16,512]{2,1,0:T(8,128)(2,1)S(1)} %get-tuple-element.68), channel_id=1, source_target_pairs={{2,0},{4,2},{6,4},{8,6},{10,8},{12,10},{14,12},{3,1},{5,3},{7,5},{... | collective-permute-start | bytes 393224 | tf_op jit(solution)/shard_map/ppermute | solution.py:15
  11.8 90.4 %collective-permute-start = (bf16[8,32,512]{2,1,0:T(8,128)(2,1)S(1)}, bf16[8,32,512]{2,1,0:T(8,128)(2,1)}, u32[]{:S(2)}, u32[]{:S(2)}) collective-permute-start(bf16[8,32,512]{2,1,0:T(8,128)(2,1)S(1)} %all_gather.3), channel_id=1, source_target_pairs={{0,2},{2,4},{4,6},{6,8},{8,10},{10,12},{12,14},{1,3},{3,5},{5,7},{... | collective-permute-start | bytes 786440 | tf_op jit(solution)/shard_map/ppermute | solution.py:15
  17.1 85.1 %collective-permute-start.1 = (bf16[8,32,512]{2,1,0:T(8,128)(2,1)S(1)}, bf16[8,32,512]{2,1,0:T(8,128)(2,1)}, u32[]{:S(2)}, u32[]{:S(2)}) collective-permute-start(bf16[8,32,512]{2,1,0:T(8,128)(2,1)S(1)} %all_gather.3), channel_id=1, source_target_pairs={{2,0},{4,2},{6,4},{8,6},{10,8},{12,10},{14,12},{3,1},{5,3},{7,5},{... | collective-permute-start | bytes 786440 | tf_op jit(solution)/shard_map/ppermute | solution.py:15
  21.8 3.7 %copy-start.60 = (pred[8]{0:T(512)(128)(4,1)}, pred[8]{0:T(512)(128)(4,1)S(1)}, u32[]{:S(2)}) copy-start(pred[8]{0:T(512)(128)(4,1)S(1)} %get-tuple-element.18) | copy-start | bytes 28
  25.0 21.6 %copy-start.71 = (pred[512]{0:T(512)(128)(4,1)}, pred[512]{0:T(512)(128)(4,1)S(1)}, u32[]{:S(2)}) copy-start(pred[512]{0:T(512)(128)(4,1)S(1)} %get-tuple-element.91) | copy-start | bytes 1540
  25.0 23.2 %copy-start.69 = (pred[512]{0:T(512)(128)(4,1)}, pred[512]{0:T(512)(128)(4,1)S(1)}, u32[]{:S(2)}) copy-start(pred[512]{0:T(512)(128)(4,1)S(1)} %get-tuple-element.90) | copy-start | bytes 1540
  26.7 4.6 %copy-start.62 = (pred[8]{0:T(512)(128)(4,1)}, pred[8]{0:T(512)(128)(4,1)S(1)}, u32[]{:S(2)}) copy-start(pred[8]{0:T(512)(128)(4,1)S(1)} %get-tuple-element.84) | copy-start | bytes 28
  26.8 14.8 %copy-start.64 = (pred[8]{0:T(512)(128)(4,1)}, pred[8]{0:T(512)(128)(4,1)S(1)}, u32[]{:S(2)}) copy-start(pred[8]{0:T(512)(128)(4,1)S(1)} %get-tuple-element.22) | copy-start | bytes 28
  26.8 3.4 %copy-start.49 = (s32[1024]{0:T(1024)}, s32[1024]{0:T(1024)S(1)}, u32[]{:S(2)}) copy-start(s32[1024]{0:T(1024)S(1)} %pad_clamp_fusion.3) | copy-start | bytes 12292
  33.7 12.7 %copy-start.56 = (pred[512]{0:T(512)(128)(4,1)}, pred[512]{0:T(512)(128)(4,1)S(1)}, u32[]{:S(2)}) copy-start(pred[512]{0:T(512)(128)(4,1)S(1)} %get-tuple-element.89) | copy-start | bytes 1540
  33.7 15.1 %copy-start.54 = (pred[512]{0:T(512)(128)(4,1)}, pred[512]{0:T(512)(128)(4,1)S(1)}, u32[]{:S(2)}) copy-start(pred[512]{0:T(512)(128)(4,1)S(1)} %get-tuple-element.88) | copy-start | bytes 1540
  39.8 1.7 %copy-start.50 = (s32[1024]{0:T(1024)}, s32[1024]{0:T(1024)S(1)}, u32[]{:S(2)}) copy-start(s32[1024]{0:T(1024)S(1)} %pad_clamp_fusion.2) | copy-start | bytes 12292
  41.8 4.0 %copy-start.11 = (bf16[1,8,32,504]{3,2,1,0:T(8,128)(2,1)S(1)}, bf16[1,8,32,504]{3,2,1,0:T(8,128)(2,1)}, u32[]{:S(2)}) copy-start(bf16[1,8,32,504]{3,2,1,0:T(8,128)(2,1)} %get-tuple-element.41) | copy-start | bytes 774148
  41.9 4.0 %copy-start.27 = (bf16[1,8,32,56]{3,2,1,0:T(8,128)(2,1)S(1)}, bf16[1,8,32,56]{3,2,1,0:T(8,128)(2,1)}, u32[]{:S(2)}) copy-start(bf16[1,8,32,56]{3,2,1,0:T(8,128)(2,1)} %slice_bitcast_fusion.27) | copy-start | bytes 86020
  41.9 4.0 %copy-start.40 = (bf16[1,8,32,8]{3,2,1,0:T(8,128)(2,1)S(1)}, bf16[1,8,32,8]{3,2,1,0:T(8,128)(2,1)}, u32[]{:S(2)}) copy-start(bf16[1,8,32,8]{3,2,1,0:T(8,128)(2,1)} %get-tuple-element.39) | copy-start | bytes 12292
  42.2 3.8 %copy-start.2 = (bf16[1,8,32,456]{3,2,1,0:T(8,128)(2,1)S(1)}, bf16[1,8,32,456]{3,2,1,0:T(8,128)(2,1)}, u32[]{:S(2)}) copy-start(bf16[1,8,32,456]{3,2,1,0:T(8,128)(2,1)} %slice_bitcast_fusion.9) | copy-start | bytes 700420
  42.2 3.8 %copy-start.12 = (bf16[1,8,32,504]{3,2,1,0:T(8,128)(2,1)S(1)}, bf16[1,8,32,504]{3,2,1,0:T(8,128)(2,1)}, u32[]{:S(2)}) copy-start(bf16[1,8,32,504]{3,2,1,0:T(8,128)(2,1)} %get-tuple-element.37) | copy-start | bytes 774148
  42.2 3.8 %copy-start.28 = (bf16[1,8,32,56]{3,2,1,0:T(8,128)(2,1)S(1)}, bf16[1,8,32,56]{3,2,1,0:T(8,128)(2,1)}, u32[]{:S(2)}) copy-start(bf16[1,8,32,56]{3,2,1,0:T(8,128)(2,1)} %slice_bitcast_fusion.25) | copy-start | bytes 86020
  42.2 3.8 %copy-start.41 = (bf16[1,8,32,8]{3,2,1,0:T(8,128)(2,1)S(1)}, bf16[1,8,32,8]{3,2,1,0:T(8,128)(2,1)}, u32[]{:S(2)}) copy-start(bf16[1,8,32,8]{3,2,1,0:T(8,128)(2,1)} %get-tuple-element.35) | copy-start | bytes 12292
  44.2 2.1 %copy-start.3 = (bf16[1,8,32,456]{3,2,1,0:T(8,128)(2,1)S(1)}, bf16[1,8,32,456]{3,2,1,0:T(8,128)(2,1)}, u32[]{:S(2)}) copy-start(bf16[1,8,32,456]{3,2,1,0:T(8,128)(2,1)} %slice_bitcast_fusion.7) | copy-start | bytes 700420
  44.2 2.1 %copy-start.13 = (bf16[1,8,32,504]{3,2,1,0:T(8,128)(2,1)S(1)}, bf16[1,8,32,504]{3,2,1,0:T(8,128)(2,1)}, u32[]{:S(2)}) copy-start(bf16[1,8,32,504]{3,2,1,0:T(8,128)(2,1)} %get-tuple-element.33) | copy-start | bytes 774148
  44.2 2.1 %copy-start.29 = (bf16[1,8,32,56]{3,2,1,0:T(8,128)(2,1)S(1)}, bf16[1,8,32,56]{3,2,1,0:T(8,128)(2,1)}, u32[]{:S(2)}) copy-start(bf16[1,8,32,56]{3,2,1,0:T(8,128)(2,1)} %slice_bitcast_fusion.23) | copy-start | bytes 86020
  44.2 2.1 %copy-start.42 = (bf16[1,8,32,8]{3,2,1,0:T(8,128)(2,1)S(1)}, bf16[1,8,32,8]{3,2,1,0:T(8,128)(2,1)}, u32[]{:S(2)}) copy-start(bf16[1,8,32,8]{3,2,1,0:T(8,128)(2,1)} %get-tuple-element.31) | copy-start | bytes 12292
  46.1 2.0 %copy-start.4 = (bf16[1,8,32,511]{3,2,1,0:T(8,128)(2,1)S(1)}, bf16[1,8,32,511]{3,2,1,0:T(8,128)(2,1)}, u32[]{:S(2)}) copy-start(bf16[1,8,32,511]{3,2,1,0:T(8,128)(2,1)} %get-tuple-element.46) | copy-start | bytes 784900
  46.1 2.0 %copy-start.25 = (bf16[1,8,32,7]{3,2,1,0:T(8,128)(2,1)S(1)}, bf16[1,8,32,7]{3,2,1,0:T(8,128)(2,1)}, u32[]{:S(2)}) copy-start(bf16[1,8,32,7]{3,2,1,0:T(8,128)(2,1)} %get-tuple-element.52) | copy-start | bytes 10756
  46.1 2.0 %copy-start.33 = (bf16[1,8,32,1]{3,2,1,0:T(8,128)(2,1)S(1)}, bf16[1,8,32,1]{3,2,1,0:T(8,128)(2,1)}, u32[]{:S(2)}) copy-start(bf16[1,8,32,1]{3,2,1,0:T(8,128)(2,1)} %get-tuple-element.42) | copy-start | bytes 1540
  46.4 1.9 %copy-start.8 = (bf16[1,8,32,504]{3,2,1,0:T(8,128)(2,1)S(1)}, bf16[1,8,32,504]{3,2,1,0:T(8,128)(2,1)}, u32[]{:S(2)}) copy-start(bf16[1,8,32,504]{3,2,1,0:T(8,128)(2,1)} %get-tuple-element.40) | copy-start | bytes 774148
  46.4 1.9 %copy-start.37 = (bf16[1,8,32,8]{3,2,1,0:T(8,128)(2,1)S(1)}, bf16[1,8,32,8]{3,2,1,0:T(8,128)(2,1)}, u32[]{:S(2)}) copy-start(bf16[1,8,32,8]{3,2,1,0:T(8,128)(2,1)} %get-tuple-element.38) | copy-start | bytes 12292
  46.6 1.9 %copy-start.9 = (bf16[1,8,32,504]{3,2,1,0:T(8,128)(2,1)S(1)}, bf16[1,8,32,504]{3,2,1,0:T(8,128)(2,1)}, u32[]{:S(2)}) copy-start(bf16[1,8,32,504]{3,2,1,0:T(8,128)(2,1)} %get-tuple-element.36) | copy-start | bytes 774148
  46.6 1.9 %copy-start.38 = (bf16[1,8,32,8]{3,2,1,0:T(8,128)(2,1)S(1)}, bf16[1,8,32,8]{3,2,1,0:T(8,128)(2,1)}, u32[]{:S(2)}) copy-start(bf16[1,8,32,8]{3,2,1,0:T(8,128)(2,1)} %get-tuple-element.34) | copy-start | bytes 12292
  46.8 1.9 %copy-start.10 = (bf16[1,8,32,504]{3,2,1,0:T(8,128)(2,1)S(1)}, bf16[1,8,32,504]{3,2,1,0:T(8,128)(2,1)}, u32[]{:S(2)}) copy-start(bf16[1,8,32,504]{3,2,1,0:T(8,128)(2,1)} %get-tuple-element.32) | copy-start | bytes 774148
  46.8 1.9 %copy-start.39 = (bf16[1,8,32,8]{3,2,1,0:T(8,128)(2,1)S(1)}, bf16[1,8,32,8]{3,2,1,0:T(8,128)(2,1)}, u32[]{:S(2)}) copy-start(bf16[1,8,32,8]{3,2,1,0:T(8,128)(2,1)} %get-tuple-element.30) | copy-start | bytes 12292
  47.5 5.9 %copy-start.67 = (pred[8]{0:T(512)(128)(4,1)}, pred[8]{0:T(512)(128)(4,1)S(1)}, u32[]{:S(2)}) copy-start(pred[8]{0:T(512)(128)(4,1)S(1)} %get-tuple-element.86) | copy-start | bytes 28
  51.1 4.8 %copy-start.15 = (bf16[8,16,448]{2,1,0:T(8,128)(2,1)S(1)}, bf16[8,16,448]{2,1,0:T(8,128)(2,1)}, u32[]{:S(2)}) copy-start(bf16[8,16,448]{2,1,0:T(8,128)(2,1)} %get-tuple-element.64) | copy-start | bytes 344068
  51.8 1.9 %copy-start.79 = (bf16[25]{0:T(256)(128)(2,1)}, bf16[25]{0:T(256)(128)(2,1)S(1)}, u32[]{:S(2)}) copy-start(bf16[25]{0:T(256)(128)(2,1)S(1)} %pad.112.clone) | copy-start | bytes 154
  51.8 1.9 %copy-start.53 = (s32[1024]{0:T(1024)}, s32[1024]{0:T(1024)S(1)}, u32[]{:S(2)}) copy-start(s32[1024]{0:T(1024)S(1)} %pad_clamp_fusion.5) | copy-start | bytes 12292
  55.0 3.3 %copy-start.14 = (bf16[8,16,448]{2,1,0:T(8,128)(2,1)S(1)}, bf16[8,16,448]{2,1,0:T(8,128)(2,1)}, u32[]{:S(2)}) copy-start(bf16[8,16,448]{2,1,0:T(8,128)(2,1)} %get-tuple-element.65) | copy-start | bytes 344068
  55.0 3.3 %copy-start.43 = (bf16[8,16,64]{2,1,0:T(8,128)(2,1)S(1)}, bf16[8,16,64]{2,1,0:T(8,128)(2,1)}, u32[]{:S(2)}) copy-start(bf16[8,16,64]{2,1,0:T(8,128)(2,1)} %slice.559) | copy-start | bytes 49156
  55.0 3.3 %copy-start.44 = (bf16[8,16,64]{2,1,0:T(8,128)(2,1)S(1)}, bf16[8,16,64]{2,1,0:T(8,128)(2,1)}, u32[]{:S(2)}) copy-start(bf16[8,16,64]{2,1,0:T(8,128)(2,1)} %get-tuple-element.63) | copy-start | bytes 49156
  55.0 3.3 %copy-start.74 = (pred[512]{0:T(512)(128)(4,1)S(1)}, pred[512]{0:T(512)(128)(4,1)}, u32[]{:S(2)}) copy-start(pred[512]{0:T(512)(128)(4,1)} %fusion.62) | copy-start | bytes 1540
  58.3 1.6 %copy-start.18 = (f32[9,16,32]{2,1,0:T(8,128)S(1)}, f32[9,16,32]{2,1,0:T(8,128)}, u32[]{:S(2)}) copy-start(f32[9,16,32]{2,1,0:T(8,128)} %convolution_bitcast_fusion.10) | copy-start | bytes 55300
  58.3 43.9 %copy-start.80 = (bf16[25]{0:T(256)(128)(2,1)S(1)}, bf16[25]{0:T(256)(128)(2,1)}, u32[]{:S(2)}) copy-start(bf16[25]{0:T(256)(128)(2,1)} %copy-done.79) | copy-start | bytes 154
  59.9 44.1 %copy-start.68 = (pred[8]{0:T(512)(128)(4,1)S(1)}, pred[8]{0:T(512)(128)(4,1)}, u32[]{:S(2)}) copy-start(pred[8]{0:T(512)(128)(4,1)} %copy-done.67) | copy-start | bytes 28
  102.2 2.9 %copy-start.66 = (pred[8]{0:T(512)(128)(4,1)S(1)}, pred[8]{0:T(512)(128)(4,1)}, u32[]{:S(2)}) copy-start(pred[8]{0:T(512)(128)(4,1)} %get-tuple-element.28) | copy-start | bytes 28
  105.5 6.3 %copy-start.19 = (bf16[1,8,32,512]{3,2,0,1:T(8,128)(2,1)}, bf16[1,8,32,512]{3,2,0,1:T(8,128)(2,1)S(1)}, u32[]{:S(2)}) copy-start(bf16[1,8,32,512]{3,2,0,1:T(8,128)(2,1)S(1)} %fusion.10) | copy-start | bytes 786436
  105.8 6.0 %copy-start.22 = (bf16[1,8,32,512]{3,2,0,1:T(8,128)(2,1)}, bf16[1,8,32,512]{3,2,0,1:T(8,128)(2,1)S(1)}, u32[]{:S(2)}) copy-start(bf16[1,8,32,512]{3,2,0,1:T(8,128)(2,1)S(1)} %fusion.11) | copy-start | bytes 786436
  107.1 2.2 %copy-start.65 = (pred[8]{0:T(512)(128)(4,1)S(1)}, pred[8]{0:T(512)(128)(4,1)}, u32[]{:S(2)}) copy-start(pred[8]{0:T(512)(128)(4,1)} %copy-done.64) | copy-start | bytes 28
  112.9 2.4 %copy-start.1 = (f32[8,16,512]{2,1,0:T(8,128)}, f32[8,16,512]{2,1,0:T(8,128)S(1)}, u32[]{:S(2)}) copy-start(f32[8,16,512]{2,1,0:T(8,128)S(1)} %convolution_bitcast_fusion.2) | copy-start | bytes 786436
  112.9 3.0 %copy-start.63 = (pred[8]{0:T(512)(128)(4,1)S(1)}, pred[8]{0:T(512)(128)(4,1)}, u32[]{:S(2)}) copy-start(pred[8]{0:T(512)(128)(4,1)} %copy-done.62) | copy-start | bytes 28
  114.5 2.6 %copy-start.55 = (pred[512]{0:T(512)(128)(4,1)S(1)}, pred[512]{0:T(512)(128)(4,1)}, u32[]{:S(2)}) copy-start(pred[512]{0:T(512)(128)(4,1)} %copy-done.54) | copy-start | bytes 1540
  114.5 2.6 %copy-start.57 = (pred[512]{0:T(512)(128)(4,1)S(1)}, pred[512]{0:T(512)(128)(4,1)}, u32[]{:S(2)}) copy-start(pred[512]{0:T(512)(128)(4,1)} %copy-done.56) | copy-start | bytes 1540
  117.4 1.9 %copy-start.61 = (pred[8]{0:T(512)(128)(4,1)S(1)}, pred[8]{0:T(512)(128)(4,1)}, u32[]{:S(2)}) copy-start(pred[8]{0:T(512)(128)(4,1)} %copy-done.60) | copy-start | bytes 28
  118.5 1.6 %copy-start.17 = (f32[8,16,512]{2,1,0:T(8,128)S(1)}, f32[8,16,512]{2,1,0:T(8,128)}, u32[]{:S(2)}) copy-start(f32[8,16,512]{2,1,0:T(8,128)} %get-tuple-element.80) | copy-start | bytes 786436
  119.4 2.1 %copy-start = (f32[8,16,512]{2,1,0:T(8,128)}, f32[8,16,512]{2,1,0:T(8,128)S(1)}, u32[]{:S(2)}) copy-start(f32[8,16,512]{2,1,0:T(8,128)S(1)} %broadcast_select_fusion.10) | copy-start | bytes 786436
  121.5 4.6 %copy-start.59 = (pred[8]{0:T(512)(128)(4,1)S(1)}, pred[8]{0:T(512)(128)(4,1)}, u32[]{:S(2)}) copy-start(pred[8]{0:T(512)(128)(4,1)} %copy-done.58) | copy-start | bytes 28
  121.6 4.8 %copy-start.16 = (f32[8,16,512]{2,1,0:T(8,128)S(1)}, f32[8,16,512]{2,1,0:T(8,128)}, u32[]{:S(2)}) copy-start(f32[8,16,512]{2,1,0:T(8,128)} %get-tuple-element.81) | copy-start | bytes 786436
  121.7 4.7 %slice-start = ((f32[8,16,512]{2,1,0:T(8,128)}), f32[8,16,7]{2,1,0:T(8,128)S(1)}, s32[]{:S(2)}) async-start(f32[8,16,512]{2,1,0:T(8,128)} %copy-done), calls=%async_computation | async-start | bytes 131072 | tf_op jit(solution)/shard_map/jit(_roll_static)/slice | solution.py:42
  121.7 4.7 %copy-start.48 = (f32[8,512]{1,0:T(8,128)S(1)}, f32[8,512]{1,0:T(8,128)}, u32[]{:S(2)}) copy-start(f32[8,512]{1,0:T(8,128)} %get-tuple-element.66) | copy-start | bytes 49156
  121.7 4.7 %copy-start.70 = (pred[512]{0:T(512)(128)(4,1)S(1)}, pred[512]{0:T(512)(128)(4,1)}, u32[]{:S(2)}) copy-start(pred[512]{0:T(512)(128)(4,1)} %copy-done.69) | copy-start | bytes 1540
  121.7 4.7 %copy-start.72 = (pred[512]{0:T(512)(128)(4,1)S(1)}, pred[512]{0:T(512)(128)(4,1)}, u32[]{:S(2)}) copy-start(pred[512]{0:T(512)(128)(4,1)} %copy-done.71) | copy-start | bytes 1540
  123.8 2.6 %copy-start.30 = (f32[8,16,456]{2,1,0:T(8,128)S(1)}, f32[8,16,456]{2,1,0:T(8,128)}, u32[]{:S(2)}) copy-start(f32[8,16,456]{2,1,0:T(8,128)} %slice.494) | copy-start | bytes 700420
  123.8 2.6 %copy-start.45 = (f32[8,16,1]{2,1,0:T(8,128)S(1)}, f32[8,16,1]{2,1,0:T(8,128)}, u32[]{:S(2)}) copy-start(f32[8,16,1]{2,1,0:T(8,128)} %slice.509) | copy-start | bytes 1540
  123.8 2.6 %copy-start.46 = (f32[8,16,56]{2,1,0:T(8,128)S(1)}, f32[8,16,56]{2,1,0:T(8,128)}, u32[]{:S(2)}) copy-start(f32[8,16,56]{2,1,0:T(8,128)} %slice.495) | copy-start | bytes 86020
  (24 other events, 26.4 us)
where the time goes:
time: 130 us; the launch traced here: 129 us
  blocking collectives  43.5 us (33%)
  local copies, waits for them, and re-layouts  38.9 us (30%)
  other arithmetic  17.4 us (13%)
  starting transfers between devices  13.3 us (10%)
  matrix products  13.2 us (10%)
  between operations  2.33 us (2%)
    psum x1, blocking collectives, local(): grad_weight = lax.psum(weight_terms, ('region', 'strip')) * scale_factor  41.5 us
    gather x20, local copies, waits for them, and re-layouts, shift_with(): jnp.take(source, row_index, axis=0)  14.2 us
    ppermute x4, starting transfers between devices, from_behind(): return lax.ppermute(block, axis, route)  13.3 us
    concatenate x10, local copies, waits for them, and re-layouts, shift_with(): own_part = jnp.roll(values_in, -offset_step * stride, axis=2)  8 us
    dot_general x9, matrix products, local(): jnp.einsum('xio,xbop->bip', tap_weights, across_grads, preferred_element_...  7.18 us
    dot_general x3, matrix products, local(): jnp.einsum('bip,sbop->sio', across_feats[index_x], cross_grads, preferred...  6.01 us
    concatenate x20, local copies, waits for them, and re-layouts, shift_with(): jnp.roll(jnp.take(source, row_index, axis=0), 7 * offset_step * stride, a...  5.91 us
    slice x15, local copies, waits for them, and re-layouts, shift_with(): own_part = jnp.roll(values_in, -offset_step * stride, axis=2)  5.66 us
  transfers between devices with their start and end apart: 4, of which 0 were waited for; matrix products, arithmetic and copies ran while one was open for 32% of the time, Pallas kernels for 0%

commit v1 on v0

v1 whole, which is shorter than its diff:
```python
import math

import jax
import jax.numpy as jnp
from jax import lax
from jax.experimental import pallas as pl
from jax.experimental.pallas import tpu as pltpu
from jax.sharding import PartitionSpec as P

GY = 4
GZ = 2
BRICKS = GY * GZ
EDGE = 8
LANES = 512
PARTS = 6
MESH = pl.DeviceIdType.MESH
LINE = ("region", "strip")


def lane_of(shape):
    return lax.broadcasted_iota(jnp.int32, shape, len(shape) - 1)


def roll(a, distance):
    return pltpu.roll(a, distance % LANES, 1)


def at_y(a, step):
    lane = lane_of(a.shape)
    row = (lane // 8) % 8
    brick = lane // 128
    if step > 0:
        near, far, other = row < 7, brick < GY - 1, 72
    else:
        near, far, other = row > 0, brick > 0, 72
    return jnp.where(
        near,
        roll(a, -8 * step),
        jnp.where(far, roll(a, -other * step), jnp.zeros_like(a)),
    )


def at_z(a, step):
    lane = lane_of(a.shape)
    column = lane % 8
    brick = (lane // 64) % 2
    if step > 0:
        near, far = column < 7, brick == 0
    else:
        near, far = column > 0, brick == 1
    return jnp.where(
        near,
        roll(a, -step),
        jnp.where(far, roll(a, -57 * step), jnp.zeros_like(a)),
    )


def planes_of(first, second):
    low = lane_of(first.shape) % 128 < 64
    even = jnp.where(low, first, roll(second, 64))
    odd = jnp.where(low, roll(first, -64), second)
    return even, odd


def kernel(
    scale,
    f_ref,
    g_ref,
    w_ref,
    occ_ref,
    nb_ref,
    gf_ref,
    gw_ref,
    grads,
    masked,
    feats,
    shifted,
    weights,
    rows,
    terms,
    arrived,
    totals,
    face_send,
    face_recv,
    part_send,
    part_recv,
    total_send,
    total_recv,
):
    strips = lax.axis_size("strip")
    count = strips * lax.axis_size("region")
    chan = lax.axis_index("chan")
    me = lax.axis_index("region") * strips + lax.axis_index("strip")
    other = 1 - chan

    def place(index, core):
        return {
            "region": lax.div(index, strips),
            "strip": lax.rem(index, strips),
            "chan": core,
        }

    def each_peer(body):
        if count <= 8:
            for j in range(1, count):
                body(lax.rem(me + j, count), j)
        else:

            def step(j, carry):
                body(lax.rem(me + j, count), j)
                return carry

            lax.fori_loop(1, count, step, 0)

    barrier = pltpu.get_barrier_semaphore()

    def greet(index, core):
        pl.semaphore_signal(
            barrier, inc=1, device_id=place(index, core), device_id_type=MESH
        )

    greet(me, other)

    @pl.when(me > 0)
    def _():
        greet(me - 1, other)

    @pl.when(me < count - 1)
    def _():
        greet(me + 1, other)

    each_peer(lambda peer, j: greet(peer, chan))

    base = me * BRICKS

    def own(entry):
        return jnp.clip(entry - base, 0, BRICKS - 1)

    corner = 0
    for b in range(BRICKS):
        corner += jnp.where((nb_ref[b, 10] < 0) & (nb_ref[b, 12] < 0), b, 0)
    slots = []
    here = corner
    for by in range(GY):
        slots.append((here, own(nb_ref[here, 14])))
        if by < GY - 1:
            here = own(nb_ref[here, 16])

    for b in range(BRICKS):
        occupied = occ_ref[b : b + 1, :].astype(jnp.float32)
        masked[b] = g_ref[b].astype(jnp.float32) * occupied
    for by in range(GY):
        even, odd = planes_of(masked[slots[by][0]], masked[slots[by][1]])
        at = slice(128 * by, 128 * (by + 1))
        for k in range(4):
            part = slice(128 * k, 128 * (k + 1))
            grads[1 + 2 * k, chan, :, at] = even[:, part].astype(jnp.bfloat16)
            grads[2 + 2 * k, chan, :, at] = odd[:, part].astype(jnp.bfloat16)

    zero_plane = jnp.zeros((2, 16, LANES), jnp.bfloat16)

    @pl.when(me == 0)
    def _():
        grads[0] = zero_plane

    @pl.when(me == count - 1)
    def _():
        grads[EDGE + 1] = zero_plane

    neighbours = 2 + (me > 0).astype(jnp.int32) + (me < count - 1).astype(jnp.int32)
    pl.semaphore_wait(barrier, count - 2 + neighbours)

    def send_plane(source, target, index, core, k, channel):
        return pltpu.make_async_remote_copy(
            src_ref=grads.at[source, channel],
            dst_ref=grads.at[target, channel],
            send_sem=face_send.at[k],
            recv_sem=face_recv.at[k],
            device_id=place(index, core),
            device_id_type=MESH,
        )

    to_next = [
        send_plane(EDGE, 0, me + 1, chan, 1, chan),
        send_plane(EDGE, 0, me + 1, other, 2, chan),
    ]
    to_last = [
        send_plane(1, EDGE + 1, me - 1, chan, 3, chan),
        send_plane(1, EDGE + 1, me - 1, other, 4, chan),
    ]
    from_last = [
        send_plane(EDGE, 0, me - 1, chan, 1, chan),
        send_plane(EDGE, 0, me - 1, other, 2, other),
    ]
    from_next = [
        send_plane(1, EDGE + 1, me + 1, chan, 3, chan),
        send_plane(1, EDGE + 1, me + 1, other, 4, other),
    ]

    @pl.when(me < count - 1)
    def _():
        for copy in to_next:
            copy.start()

    @pl.when(me > 0)
    def _():
        for copy in to_last:
            copy.start()

    swap = send_plane(pl.ds(1, EDGE), pl.ds(1, EDGE), me, other, 0, chan)
    swap.start()
    swap_in = send_plane(pl.ds(1, EDGE), pl.ds(1, EDGE), me, other, 0, other)

    for b in range(BRICKS):
        occupied = occ_ref[b : b + 1, :].astype(jnp.float32)
        masked[b] = f_ref[b].astype(jnp.float32) * occupied
    for by in range(GY):
        even, odd = planes_of(masked[slots[by][0]], masked[slots[by][1]])
        at = slice(128 * by, 128 * (by + 1))
        for k in range(4):
            part = slice(128 * k, 128 * (k + 1))
            feats[2 * k, :, at] = even[:, part]
            feats[2 * k + 1, :, at] = odd[:, part]
    for x in range(EDGE):
        plane = feats[x]
        depth = jnp.concatenate([at_z(plane, -1), plane, at_z(plane, 1)], axis=0)
        shifted[x, 0:48] = at_y(depth, -1).astype(jnp.bfloat16)
        shifted[x, 48:96] = depth.astype(jnp.bfloat16)
        shifted[x, 96:144] = at_y(depth, 1).astype(jnp.bfloat16)
    for a in range(3):
        weights[:, 32 * a : 32 * (a + 1)] = w_ref[9 * a : 9 * (a + 1)].reshape(144, 32)

    def window(x):
        return jnp.concatenate(
            [grads[x + 2 - a].reshape(32, LANES) for a in range(3)], axis=0
        )

    def term(x):
        return lax.dot_general(
            shifted[x],
            window(x),
            (((1,), (1,)), ((), ())),
            preferred_element_type=jnp.float32,
        )

    swap_in.wait_recv()
    total = term(1)
    for x in range(2, EDGE - 1):
        total = total + term(x)

    @pl.when(me > 0)
    def _():
        for copy in from_last:
            copy.wait_recv()

    @pl.when(me < count - 1)
    def _():
        for copy in from_next:
            copy.wait_recv()

    total = total + term(0) + term(EDGE - 1)
    terms[...] = total.reshape(terms.shape)

    def give(q, source):
        return pltpu.make_async_remote_copy(
            src_ref=terms.at[q],
            dst_ref=arrived.at[source],
            send_sem=part_send.at[q],
            recv_sem=part_recv.at[source],
            device_id=place(q, chan),
            device_id_type=MESH,
        )

    for q in range(PARTS):

        @pl.when(me != q)
        def _():
            give(q, me).start()

    for x in range(EDGE):
        taps = jnp.dot(weights[...], window(x), preferred_element_type=jnp.float32)
        depth = taps[48:96] + at_y(taps[0:48], 1) + at_y(taps[96:144], -1)
        feats[x] = depth[16:32] + at_z(depth[0:16], 1) + at_z(depth[32:48], -1)
    for by in range(GY):
        at = slice(128 * by, 128 * (by + 1))
        even = jnp.concatenate([feats[2 * k, :, at] for k in range(4)], axis=1)
        odd = jnp.concatenate([feats[2 * k + 1, :, at] for k in range(4)], axis=1)
        first, second = planes_of(even, odd)
        rows[GZ * by] = first
        rows[GZ * by + 1] = second
    for b in range(BRICKS):
        below = nb_ref[b, 10]
        two_below = nb_ref[own(below), 10]
        y = jnp.where(
            below < 0,
            0,
            jnp.where(two_below < 0, 1, jnp.where(nb_ref[b, 16] >= 0, 2, 3)),
        )
        z = jnp.where(nb_ref[b, 12] >= 0, 1, 0)
        occupied = occ_ref[b : b + 1, :].astype(jnp.float32)
        gf_ref[b] = (rows[GZ * y + z] * occupied).astype(jnp.bfloat16)

    def share(owner, target):
        return pltpu.make_async_remote_copy(
            src_ref=totals.at[owner],
            dst_ref=totals.at[owner],
            send_sem=total_send.at[target],
            recv_sem=total_recv.at[owner],
            device_id=place(target, chan),
            device_id_type=MESH,
        )

    @pl.when(me < PARTS)
    def _():
        each_peer(lambda peer, j: give(me, peer).wait_recv())
        arrived[me] = terms[me]

        def add(j, carry):
            return carry + arrived[j]

        if count <= 8:
            result = arrived[0]
            for j in range(1, count):
                result = add(j, result)
        else:
            result = lax.fori_loop(1, count, add, arrived[0])
        totals[me] = result * scale
        each_peer(lambda peer, j: share(me, peer).start())

    for q in range(PARTS):

        @pl.when(me != q)
        def _():
            share(q, q).wait_recv()

    whole = totals[...].reshape(144, 96)
    for a in range(3):
        gw_ref[9 * a : 9 * (a + 1)] = whole[:, 32 * a : 32 * (a + 1)].reshape(9, 16, 32)

    @pl.when(me < PARTS)
    def _():
        each_peer(lambda peer, j: share(me, peer).wait_send())

    for q in range(PARTS):

        @pl.when(me != q)
        def _():
            give(q, me).wait_send()

    swap.wait_send()

    @pl.when(me < count - 1)
    def _():
        for copy in to_next:
            copy.wait_send()

    @pl.when(me > 0)
    def _():
        for copy in to_last:
            copy.wait_send()


def local(features, out_grad, weight, occupancy, neighbours):
    count = lax.axis_size(LINE)
    scale = 1.0 / math.sqrt(features.shape[0] * count * LANES)
    part = (24, 96)
    vmem = pl.BlockSpec(memory_space=pltpu.VMEM)

    def body(*refs):
        kernel(scale, *refs)

    return pl.pallas_call(
        body,
        out_shape=(
            jax.ShapeDtypeStruct(features.shape, jnp.bfloat16),
            jax.ShapeDtypeStruct(weight.shape, jnp.float32),
        ),
        in_specs=[vmem, vmem, vmem, vmem, pl.BlockSpec(memory_space=pltpu.SMEM)],
        out_specs=(vmem, vmem),
        scratch_shapes=[
            pltpu.VMEM((EDGE + 2, 2, 16, LANES), jnp.bfloat16),
            pltpu.VMEM((BRICKS, 16, LANES), jnp.float32),
            pltpu.VMEM((EDGE, 16, LANES), jnp.float32),
            pltpu.VMEM((EDGE, 144, LANES), jnp.bfloat16),
            pltpu.VMEM((144, 96), jnp.bfloat16),
            pltpu.VMEM((BRICKS, 16, LANES), jnp.float32),
            pltpu.VMEM((PARTS,) + part, jnp.float32),
            pltpu.VMEM((count,) + part, jnp.float32),
            pltpu.VMEM((PARTS,) + part, jnp.float32),
            pltpu.SemaphoreType.DMA((5,)),
            pltpu.SemaphoreType.DMA((5,)),
            pltpu.SemaphoreType.DMA((PARTS,)),
            pltpu.SemaphoreType.DMA((count,)),
            pltpu.SemaphoreType.DMA((count,)),
            pltpu.SemaphoreType.DMA((PARTS,)),
        ],
        compiler_params=pltpu.CompilerParams(
            collective_id=0, has_side_effects=True, vmem_limit_bytes=32 * 1024 * 1024
        ),
        name="brick_conv_backward",
    )(features, out_grad, weight, occupancy, neighbours)


def solution(mesh):
    rows = P(("groups", "region", "strip"), "chan", None)
    tables = P(("groups", "region", "strip"), None)
    return jax.shard_map(
        local,
        mesh=mesh,
        in_specs=(rows, rows, P(None, "chan", None), tables, tables),
        out_specs=(rows, P("groups", "chan", None)),
        check_vma=False,
    )
```

time: 130 us -> 24.1 us (0.19)
  blocking collectives: 43.5 us -> 0 us
  local copies, waits for them, and re-layouts: 38.9 us -> 5.44 us
  Pallas kernels: 0 us -> 17.7 us
  other arithmetic: 17.4 us -> 0 us
  starting transfers between devices: 13.3 us -> 0 us
  matrix products: 13.2 us -> 0 us
  between operations: 2.33 us -> 0.65 us
    psum x1 -> x0, blocking collectives: 41.5 us -> none  [local(): grad_weight = lax.psum(weight_terms, ('region', 'strip')) * scale_factor]
    pallas_call x0 -> x1, Pallas kernels: none -> 17.7 us  [local(): pl.pallas_call(body, out_shape=(jax.ShapeDtypeStruct(features.shape, jnp....]
    concatenate x42 -> x0, local copies, waits for them, and re-layouts: 14.2 us -> none  [the longest x10 8 us: shift_with(): own_part = jnp.roll(values_in, -offset_step * stride, axis=2)]
    gather x20 -> x0, local copies, waits for them, and re-layouts: 14.2 us -> none  [shift_with(): jnp.take(source, row_index, axis=0)]
    ppermute x4 -> x0, starting transfers between devices: 13.3 us -> none  [from_behind(): return lax.ppermute(block, axis, route)]
    dot_general x12 -> x0, matrix products: 13.2 us -> none  [the longest x9 7.18 us: local(): jnp.einsum('xio,xbop->bip', tap_weights, across_grads, preferred_element_...]
    slice x31 -> x0, local copies, waits for them, and re-layouts: 9.43 us -> none  [the longest x15 5.66 us: shift_with(): own_part = jnp.roll(values_in, -offset_step * stride, axis=2)]
    select_n x16 -> x0, other arithmetic: 4.7 us -> none  [the longest x12 3.91 us: shift_with(): jnp.take(source, row_index, axis=0)]
  transfers between devices with their start and end apart: 4 -> 0, of which waited for: 0 -> 0; matrix products, arithmetic and copies ran while one was open for 32% -> 0% of each run, Pallas kernels for 0% -> 0%
where the time goes in v1:
time: 24.1 us; the launch traced here: 23.8 us
  Pallas kernels  17.7 us (73%)
  local copies, waits for them, and re-layouts  5.44 us (23%)
  between operations  0.65 us (3%)
    pallas_call x1, Pallas kernels, local(): pl.pallas_call(body, out_shape=(jax.ShapeDtypeStruct(features.shape, jnp....  17.7 us
    unnamed x12, local copies, waits for them, and re-layouts  5.44 us

profile of v1, /device:TPU:0, one launch (start us, length us, event | category | flops | bytes accessed | tf_op | source)
XLA Modules:
  0.0 23.8 jit_solution(16673379517612273373)
XLA Ops:
  0.6 0.0 copy-start
  0.6 0.9 %copy-done = bf16[8,16,512]{2,1,0:T(8,128)(2,1)S(1)} copy-done((bf16[8,16,512]{2,1,0:T(8,128)(2,1)S(1)}, bf16[8,16,512]{2,1,0:T(8,128)(2,1)}, u32[]{:S(2)}) %copy-start) | copy-done | bytes 131096
  1.5 0.0 copy-start.1
  1.5 0.9 %copy-done.1 = bf16[8,16,512]{2,1,0:T(8,128)(2,1)S(1)} copy-done((bf16[8,16,512]{2,1,0:T(8,128)(2,1)S(1)}, bf16[8,16,512]{2,1,0:T(8,128)(2,1)}, u32[]{:S(2)}) %copy-start.1) | copy-done | bytes 131096
  2.4 0.0 copy-start.2
  2.4 0.9 %copy-done.2 = bf16[27,16,32]{2,1,0:T(8,128)(2,1)S(1)} copy-done((bf16[27,16,32]{2,1,0:T(8,128)(2,1)S(1)}, bf16[27,16,32]{2,1,0:T(8,128)(2,1)}, u32[]{:S(2)}) %copy-start.2) | copy-done | bytes 27672
  3.3 0.0 copy-start.3
  3.3 0.7 %copy-done.3 = s32[8,512]{1,0:T(8,128)S(1)} copy-done((s32[8,512]{1,0:T(8,128)S(1)}, s32[8,512]{1,0:T(8,128)}, u32[]{:S(2)}) %copy-start.3) | copy-done | bytes 16408
  4.1 0.0 copy-start.4
  4.1 0.7 %copy-done.4 = s32[8,27]{1,0:T(8,128)S(1)} copy-done((s32[8,27]{1,0:T(8,128)S(1)}, s32[8,27]{1,0:T(8,128)}, u32[]{:S(2)}) %copy-start.4) | copy-done | bytes 888
  4.7 17.7 %brick_conv_backward.1 = (bf16[8,16,512]{2,1,0:T(8,128)(2,1)S(1)}, f32[27,16,32]{2,1,0:T(8,128)S(1)}) custom-call(bf16[8,16,512]{2,1,0:T(8,128)(2,1)S(1)} %copy-done, bf16[8,16,512]{2,1,0:T(8,128)(2,1)S(1)} %copy-done.1, bf16[27,16,32]{2,1,0:T(8,128)(2,1)S(1)} %copy-done.2, s32[8,512]{1,0:T(8,128)S(1)} %copy-done.3, s32[8,27]{1,0:T(8,128)S(1)} %copy-done.4), custom_call_target="tpu_custom_call" | custom-call | tf_op jit(solution)/shard_map/brick_conv_backward/pallas_call | solution.py:372
  22.4 0.7 %copy.9 = bf16[8,16,512]{2,1,0:T(8,128)(2,1)} copy(bf16[8,16,512]{2,1,0:T(8,128)(2,1)S(1)} %get-tuple-element.4) | data formatting | bytes 262144
  23.1 0.7 %copy.10 = f32[27,16,32]{2,1,0:T(8,128)} copy(f32[27,16,32]{2,1,0:T(8,128)S(1)} %get-tuple-element.5) | data formatting | bytes 110592
Async XLA Ops:
  0.6 0.9 %copy-start = (bf16[8,16,512]{2,1,0:T(8,128)(2,1)S(1)}, bf16[8,16,512]{2,1,0:T(8,128)(2,1)}, u32[]{:S(2)}) copy-start(bf16[8,16,512]{2,1,0:T(8,128)(2,1)} %refs_0_.1) | copy-start | bytes 393220
  1.5 0.9 %copy-start.1 = (bf16[8,16,512]{2,1,0:T(8,128)(2,1)S(1)}, bf16[8,16,512]{2,1,0:T(8,128)(2,1)}, u32[]{:S(2)}) copy-start(bf16[8,16,512]{2,1,0:T(8,128)(2,1)} %refs_1_.1) | copy-start | bytes 393220
  2.4 0.9 %copy-start.2 = (bf16[27,16,32]{2,1,0:T(8,128)(2,1)S(1)}, bf16[27,16,32]{2,1,0:T(8,128)(2,1)}, u32[]{:S(2)}) copy-start(bf16[27,16,32]{2,1,0:T(8,128)(2,1)} %refs_2_.1) | copy-start | bytes 82948
  3.3 0.7 %copy-start.3 = (s32[8,512]{1,0:T(8,128)S(1)}, s32[8,512]{1,0:T(8,128)}, u32[]{:S(2)}) copy-start(s32[8,512]{1,0:T(8,128)} %refs_3_.1) | copy-start | bytes 49156
  4.1 0.7 %copy-start.4 = (s32[8,27]{1,0:T(8,128)S(1)}, s32[8,27]{1,0:T(8,128)}, u32[]{:S(2)}) copy-start(s32[8,27]{1,0:T(8,128)} %refs_4_.1) | copy-start | bytes 2596

commit v2 on v1

--- a/solution.py
+++ b/solution.py
@@ -64,13 +64,19 @@
 
 def kernel(
     scale,
+    f_in,
+    g_in,
+    w_in,
+    occ_in,
+    nb_in,
+    gf_ref,
+    gw_ref,
     f_ref,
     g_ref,
     w_ref,
     occ_ref,
     nb_ref,
-    gf_ref,
-    gw_ref,
+    load_sem,
     grads,
     masked,
     feats,
@@ -112,6 +118,20 @@
 
             lax.fori_loop(1, count, step, 0)
 
+    pairs = (
+        (nb_in, nb_ref),
+        (occ_in, occ_ref),
+        (g_in, g_ref),
+        (f_in, f_ref),
+        (w_in, w_ref),
+    )
+    loads = [
+        pltpu.make_async_copy(source, target, load_sem.at[k])
+        for k, (source, target) in enumerate(pairs)
+    ]
+    for load in loads:
+        load.start()
+
     barrier = pltpu.get_barrier_semaphore()
 
     def greet(index, core):
@@ -136,6 +156,7 @@
     def own(entry):
         return jnp.clip(entry - base, 0, BRICKS - 1)
 
+    loads[0].wait()
     corner = 0
     for b in range(BRICKS):
         corner += jnp.where((nb_ref[b, 10] < 0) & (nb_ref[b, 12] < 0), b, 0)
@@ -146,6 +167,8 @@
         if by < GY - 1:
             here = own(nb_ref[here, 16])
 
+    loads[1].wait()
+    loads[2].wait()
     for b in range(BRICKS):
         occupied = occ_ref[b : b + 1, :].astype(jnp.float32)
         masked[b] = g_ref[b].astype(jnp.float32) * occupied
@@ -211,6 +234,7 @@
     swap.start()
     swap_in = send_plane(pl.ds(1, EDGE), pl.ds(1, EDGE), me, other, 0, other)
 
+    loads[3].wait()
     for b in range(BRICKS):
         occupied = occ_ref[b : b + 1, :].astype(jnp.float32)
         masked[b] = f_ref[b].astype(jnp.float32) * occupied
@@ -227,6 +251,7 @@
         shifted[x, 0:48] = at_y(depth, -1).astype(jnp.bfloat16)
         shifted[x, 48:96] = depth.astype(jnp.bfloat16)
         shifted[x, 96:144] = at_y(depth, 1).astype(jnp.bfloat16)
+    loads[4].wait()
     for a in range(3):
         weights[:, 32 * a : 32 * (a + 1)] = w_ref[9 * a : 9 * (a + 1)].reshape(144, 32)
 
@@ -375,9 +400,15 @@
             jax.ShapeDtypeStruct(features.shape, jnp.bfloat16),
             jax.ShapeDtypeStruct(weight.shape, jnp.float32),
         ),
-        in_specs=[vmem, vmem, vmem, vmem, pl.BlockSpec(memory_space=pltpu.SMEM)],
+        in_specs=[pl.BlockSpec(memory_space=pltpu.HBM)] * 5,
         out_specs=(vmem, vmem),
         scratch_shapes=[
+            pltpu.VMEM(features.shape, jnp.bfloat16),
+            pltpu.VMEM(out_grad.shape, jnp.bfloat16),
+            pltpu.VMEM(weight.shape, jnp.bfloat16),
+            pltpu.VMEM(occupancy.shape, jnp.int32),
+            pltpu.SMEM(neighbours.shape, jnp.int32),
+            pltpu.SemaphoreType.DMA((5,)),
             pltpu.VMEM((EDGE + 2, 2, 16, LANES), jnp.bfloat16),
             pltpu.VMEM((BRICKS, 16, LANES), jnp.float32),
             pltpu.VMEM((EDGE, 16, LANES), jnp.float32),
@@ -395,7 +426,7 @@
             pltpu.SemaphoreType.DMA((PARTS,)),
         ],
         compiler_params=pltpu.CompilerParams(
-            collective_id=0, has_side_effects=True, vmem_limit_bytes=32 * 1024 * 1024
+            collective_id=0, has_side_effects=True, vmem_limit_bytes=60 * 1024 * 1024
         ),
         name="brick_conv_backward",
     )(features, out_grad, weight, occupancy, neighbours)

time: 24.1 us -> 21 us (0.87)
  local copies, waits for them, and re-layouts: 5.44 us -> 2.3 us
    unnamed x12 -> x4, local copies, waits for them, and re-layouts: 5.44 us -> 2.3 us
where the time goes in v2:
time: 21 us; the launch traced here: 20.8 us
  Pallas kernels  17.9 us (85%)
  local copies, waits for them, and re-layouts  2.3 us (11%)
  between operations  0.65 us (3%)
    pallas_call x1, Pallas kernels, local(): pl.pallas_call(body, out_shape=(jax.ShapeDtypeStruct(features.shape, jnp....  17.9 us
    unnamed x4, local copies, waits for them, and re-layouts  2.3 us

profile of v2, /device:TPU:0, one launch (start us, length us, event | category | flops | bytes accessed | tf_op | source)
XLA Modules:
  0.0 20.8 jit_solution(9502773791050646655)
XLA Ops:
  0.6 17.9 %brick_conv_backward.1 = (bf16[8,16,512]{2,1,0:T(8,128)(2,1)}, f32[27,16,32]{2,1,0:T(8,128)}) custom-call(bf16[8,16,512]{2,1,0:T(8,128)(2,1)} %refs_0_.1, bf16[8,16,512]{2,1,0:T(8,128)(2,1)} %refs_1_.1, bf16[27,16,32]{2,1,0:T(8,128)(2,1)} %refs_2_.1, s32[8,512]{1,0:T(8,128)} %refs_3_.1, s32[8,27]{1,0:T(8,128)} %refs_4_.1), custom_call_target="tpu_custom_call" | custom-call | tf_op jit(solution)/shard_map/brick_conv_backward/pallas_call | solution.py:397
  18.5 0.0 copy-start
  18.5 1.6 %copy.9 = bf16[8,16,512]{2,1,0:T(8,128)(2,1)} copy(bf16[8,16,512]{2,1,0:T(8,128)(2,1)} %get-tuple-element.4) | data formatting | bytes 262144
  20.1 0.0 copy-done
  20.1 0.7 %copy.10 = f32[27,16,32]{2,1,0:T(8,128)} copy(f32[27,16,32]{2,1,0:T(8,128)S(1)} %copy-done) | data formatting | bytes 110592
Async XLA Ops:
  18.5 1.6 %copy-start = (f32[27,16,32]{2,1,0:T(8,128)S(1)}, f32[27,16,32]{2,1,0:T(8,128)}, u32[]{:S(2)}) copy-start(f32[27,16,32]{2,1,0:T(8,128)} %get-tuple-element.5) | copy-start | bytes 165892

commit v3 on v2

--- a/solution.py
+++ b/solution.py
@@ -12,7 +12,8 @@
 BRICKS = GY * GZ
 EDGE = 8
 LANES = 512
-PARTS = 6
+PARTS = 4
+PART_ROWS = 40
 MESH = pl.DeviceIdType.MESH
 LINE = ("region", "strip")
 
@@ -69,8 +70,11 @@
     w_in,
     occ_in,
     nb_in,
+    gf_out,
+    gw_out,
     gf_ref,
     gw_ref,
+    store_sem,
     f_ref,
     g_ref,
     w_ref,
@@ -98,6 +102,10 @@
     chan = lax.axis_index("chan")
     me = lax.axis_index("region") * strips + lax.axis_index("strip")
     other = 1 - chan
+    first = (count - PARTS) // 2
+
+    def owns(index):
+        return (index >= first) & (index < first + PARTS)
 
     def place(index, core):
         return {
@@ -117,6 +125,45 @@
                 return carry
 
             lax.fori_loop(1, count, step, 0)
+
+    barrier = pltpu.get_barrier_semaphore()
+
+    def greet(index, core):
+        pl.semaphore_signal(
+            barrier, inc=1, device_id=place(index, core), device_id_type=MESH
+        )
+
+    below, above = me > 0, me < count - 1
+    plain = jnp.logical_not(owns(me))
+    meet_below = below & plain & jnp.logical_not(owns(me - 1))
+    meet_above = above & plain & jnp.logical_not(owns(me + 1))
+
+    @pl.when(owns(me))
+    def _():
+        each_peer(lambda peer, j: greet(peer, chan))
+
+    @pl.when(plain)
+    def _():
+        for q in range(PARTS):
+            greet(first + q, chan)
+
+    @pl.when(meet_below)
+    def _():
+        greet(me - 1, chan)
+
+    @pl.when(meet_above)
+    def _():
+        greet(me + 1, chan)
+
+    @pl.when(below)
+    def _():
+        greet(me - 1, other)
+
+    @pl.when(above)
+    def _():
+        greet(me + 1, other)
+
+    greet(me, other)
 
     pairs = (
         (nb_in, nb_ref),
@@ -131,25 +178,6 @@
     ]
     for load in loads:
         load.start()
-
-    barrier = pltpu.get_barrier_semaphore()
-
-    def greet(index, core):
-        pl.semaphore_signal(
-            barrier, inc=1, device_id=place(index, core), device_id_type=MESH
-        )
-
-    greet(me, other)
-
-    @pl.when(me > 0)
-    def _():
-        greet(me - 1, other)
-
-    @pl.when(me < count - 1)
-    def _():
-        greet(me + 1, other)
-
-    each_peer(lambda peer, j: greet(peer, chan))
 
     base = me * BRICKS
 
@@ -190,8 +218,10 @@
     def _():
         grads[EDGE + 1] = zero_plane
 
-    neighbours = 2 + (me > 0).astype(jnp.int32) + (me < count - 1).astype(jnp.int32)
-    pl.semaphore_wait(barrier, count - 2 + neighbours)
+    met = jnp.where(plain, PARTS, count - 1) + 1
+    for more in (below, above, meet_below, meet_above):
+        met = met + more.astype(jnp.int32)
+    pl.semaphore_wait(barrier, met)
 
     def send_plane(source, target, index, core, k, channel):
         return pltpu.make_async_remote_copy(
@@ -284,7 +314,9 @@
             copy.wait_recv()
 
     total = total + term(0) + term(EDGE - 1)
-    terms[...] = total.reshape(terms.shape)
+    for q in range(PARTS):
+        part = total[PART_ROWS * q : PART_ROWS * (q + 1)]
+        terms[q, 0 : part.shape[0]] = part
 
     def give(q, source):
         return pltpu.make_async_remote_copy(
@@ -292,13 +324,13 @@
             dst_ref=arrived.at[source],
             send_sem=part_send.at[q],
             recv_sem=part_recv.at[source],
-            device_id=place(q, chan),
+            device_id=place(first + q, chan),
             device_id_type=MESH,
         )
 
     for q in range(PARTS):
 
-        @pl.when(me != q)
+        @pl.when(me != first + q)
         def _():
             give(q, me).start()
 
@@ -310,20 +342,21 @@
         at = slice(128 * by, 128 * (by + 1))
         even = jnp.concatenate([feats[2 * k, :, at] for k in range(4)], axis=1)
         odd = jnp.concatenate([feats[2 * k + 1, :, at] for k in range(4)], axis=1)
-        first, second = planes_of(even, odd)
-        rows[GZ * by] = first
-        rows[GZ * by + 1] = second
+        rows[GZ * by], rows[GZ * by + 1] = planes_of(even, odd)
     for b in range(BRICKS):
-        below = nb_ref[b, 10]
-        two_below = nb_ref[own(below), 10]
+        left = nb_ref[b, 10]
+        next_left = nb_ref[own(left), 10]
         y = jnp.where(
-            below < 0,
+            left < 0,
             0,
-            jnp.where(two_below < 0, 1, jnp.where(nb_ref[b, 16] >= 0, 2, 3)),
+            jnp.where(next_left < 0, 1, jnp.where(nb_ref[b, 16] >= 0, 2, 3)),
         )
         z = jnp.where(nb_ref[b, 12] >= 0, 1, 0)
         occupied = occ_ref[b : b + 1, :].astype(jnp.float32)
         gf_ref[b] = (rows[GZ * y + z] * occupied).astype(jnp.bfloat16)
+
+    gf_store = pltpu.make_async_copy(gf_ref, gf_out, store_sem.at[0])
+    gf_store.start()
 
     def share(owner, target):
         return pltpu.make_async_remote_copy(
@@ -335,10 +368,12 @@
             device_id_type=MESH,
         )
 
-    @pl.when(me < PARTS)
-    def _():
-        each_peer(lambda peer, j: give(me, peer).wait_recv())
-        arrived[me] = terms[me]
+    mine = me - first
+
+    @pl.when(owns(me))
+    def _():
+        each_peer(lambda peer, j: give(mine, peer).wait_recv())
+        arrived[me] = terms[mine]
 
         def add(j, carry):
             return carry + arrived[j]
@@ -349,26 +384,28 @@
                 result = add(j, result)
         else:
             result = lax.fori_loop(1, count, add, arrived[0])
-        totals[me] = result * scale
-        each_peer(lambda peer, j: share(me, peer).start())
+        totals[mine] = result * scale
+        each_peer(lambda peer, j: share(mine, peer).start())
 
     for q in range(PARTS):
 
-        @pl.when(me != q)
+        @pl.when(me != first + q)
         def _():
-            share(q, q).wait_recv()
-
-    whole = totals[...].reshape(144, 96)
+            share(q, first + q).wait_recv()
+
+    whole = totals[...].reshape(PARTS * PART_ROWS, 96)[0:144]
     for a in range(3):
         gw_ref[9 * a : 9 * (a + 1)] = whole[:, 32 * a : 32 * (a + 1)].reshape(9, 16, 32)
-
-    @pl.when(me < PARTS)
-    def _():
-        each_peer(lambda peer, j: share(me, peer).wait_send())
+    gw_store = pltpu.make_async_copy(gw_ref, gw_out, store_sem.at[1])
+    gw_store.start()
+
+    @pl.when(owns(me))
+    def _():
+        each_peer(lambda peer, j: share(mine, peer).wait_send())
 
     for q in range(PARTS):
 
-        @pl.when(me != q)
+        @pl.when(me != first + q)
         def _():
             give(q, me).wait_send()
 
@@ -383,26 +420,53 @@
     def _():
         for copy in to_last:
             copy.wait_send()
+
+    gf_store.wait()
+    gw_store.wait()
+
+
+def deliver(gf_in, gw_in, gf_out, gw_out, gf_ref, gw_ref, sem):
+    steps = ((gf_in, gf_ref, gf_out), (gw_in, gw_ref, gw_out))
+    loads = [
+        pltpu.make_async_copy(source, held, sem.at[0, k])
+        for k, (source, held, _) in enumerate(steps)
+    ]
+    stores = [
+        pltpu.make_async_copy(held, target, sem.at[1, k])
+        for k, (_, held, target) in enumerate(steps)
+    ]
+    for load in loads:
+        load.start()
+    for load, store in zip(loads, stores):
+        load.wait()
+        store.start()
+    for store in stores:
+        store.wait()
 
 
 def local(features, out_grad, weight, occupancy, neighbours):
     count = lax.axis_size(LINE)
     scale = 1.0 / math.sqrt(features.shape[0] * count * LANES)
-    part = (24, 96)
-    vmem = pl.BlockSpec(memory_space=pltpu.VMEM)
+    part = (PART_ROWS, 96)
+    hbm = pl.BlockSpec(memory_space=pltpu.HBM)
+    outs = (
+        jax.ShapeDtypeStruct(features.shape, jnp.bfloat16),
+        jax.ShapeDtypeStruct(weight.shape, jnp.float32),
+    )
+    limit = 60 * 1024 * 1024
 
     def body(*refs):
         kernel(scale, *refs)
 
-    return pl.pallas_call(
+    results = pl.pallas_call(
         body,
-        out_shape=(
-            jax.ShapeDtypeStruct(features.shape, jnp.bfloat16),
-            jax.ShapeDtypeStruct(weight.shape, jnp.float32),
-        ),
-        in_specs=[pl.BlockSpec(memory_space=pltpu.HBM)] * 5,
-        out_specs=(vmem, vmem),
+        out_shape=outs,
+        in_specs=[hbm] * 5,
+        out_specs=(hbm, hbm),
         scratch_shapes=[
+            pltpu.VMEM(features.shape, jnp.bfloat16),
+            pltpu.VMEM(weight.shape, jnp.float32),
+            pltpu.SemaphoreType.DMA((2,)),
             pltpu.VMEM(features.shape, jnp.bfloat16),
             pltpu.VMEM(out_grad.shape, jnp.bfloat16),
             pltpu.VMEM(weight.shape, jnp.bfloat16),
@@ -426,10 +490,23 @@
             pltpu.SemaphoreType.DMA((PARTS,)),
         ],
         compiler_params=pltpu.CompilerParams(
-            collective_id=0, has_side_effects=True, vmem_limit_bytes=60 * 1024 * 1024
+            collective_id=0, has_side_effects=True, vmem_limit_bytes=limit
         ),
         name="brick_conv_backward",
     )(features, out_grad, weight, occupancy, neighbours)
+    return pl.pallas_call(
+        deliver,
+        out_shape=outs,
+        in_specs=[hbm, hbm],
+        out_specs=(hbm, hbm),
+        scratch_shapes=[
+            pltpu.VMEM(features.shape, jnp.bfloat16),
+            pltpu.VMEM(weight.shape, jnp.float32),
+            pltpu.SemaphoreType.DMA((2, 2)),
+        ],
+        compiler_params=pltpu.CompilerParams(vmem_limit_bytes=limit),
+        name="deliver",
+    )(*results)
 
 
 def solution(mesh):

time: 21 us -> 20.6 us (0.981)
  local copies, waits for them, and re-layouts: 2.3 us -> 0 us
  Pallas kernels: 17.9 us -> 19.8 us
    unnamed x4 -> x0, local copies, waits for them, and re-layouts: 2.3 us -> none
    pallas_call x1 -> x2, Pallas kernels: 17.9 us -> 19.8 us  [the longest x1 18.1 us: local(): pl.pallas_call(body, out_shape=outs, in_specs=[hbm] * 5, out_specs=(hbm,...]
where the time goes in v3:
time: 20.6 us; the launch traced here: 20.4 us
  Pallas kernels  19.8 us (96%)
  between operations  0.64 us (3%)
    pallas_call x1, Pallas kernels, local(): pl.pallas_call(body, out_shape=outs, in_specs=[hbm] * 5, out_specs=(hbm,...  18.1 us
    pallas_call x1, Pallas kernels, local(): pl.pallas_call(deliver, out_shape=outs, in_specs=[hbm, hbm], out_specs=(h...  1.72 us

profile of v3, /device:TPU:0, one launch (start us, length us, event | category | flops | bytes accessed | tf_op | source)
XLA Modules:
  0.0 20.4 jit_solution(13781176895567439695)
XLA Ops:
  0.6 18.1 %brick_conv_backward.1 = (bf16[8,16,512]{2,1,0:T(8,128)(2,1)}, f32[27,16,32]{2,1,0:T(8,128)}) custom-call(bf16[8,16,512]{2,1,0:T(8,128)(2,1)} %refs_0_.1, bf16[8,16,512]{2,1,0:T(8,128)(2,1)} %refs_1_.1, bf16[27,16,32]{2,1,0:T(8,128)(2,1)} %refs_2_.1, s32[8,512]{1,0:T(8,128)} %refs_3_.1, s32[8,27]{1,0:T(8,128)} %refs_4_.1), custom_call_target="tpu_custom_call" | custom-call | tf_op jit(solution)/shard_map/brick_conv_backward/pallas_call | solution.py:461
  18.7 1.7 %deliver.1 = (bf16[8,16,512]{2,1,0:T(8,128)(2,1)}, f32[27,16,32]{2,1,0:T(8,128)}) custom-call(bf16[8,16,512]{2,1,0:T(8,128)(2,1)} %get-tuple-element.4.gf_in, f32[27,16,32]{2,1,0:T(8,128)} %get-tuple-element.5.gw_in), custom_call_target="tpu_custom_call" | custom-call | tf_op jit(solution)/shard_map/deliver/pallas_call | solution.py:497

commit v4 on v3

--- a/solution.py
+++ b/solution.py
@@ -71,9 +71,8 @@
     occ_in,
     nb_in,
     gf_out,
-    gw_out,
+    sum_out,
     gf_ref,
-    gw_ref,
     store_sem,
     f_ref,
     g_ref,
@@ -393,11 +392,8 @@
         def _():
             share(q, first + q).wait_recv()
 
-    whole = totals[...].reshape(PARTS * PART_ROWS, 96)[0:144]
-    for a in range(3):
-        gw_ref[9 * a : 9 * (a + 1)] = whole[:, 32 * a : 32 * (a + 1)].reshape(9, 16, 32)
-    gw_store = pltpu.make_async_copy(gw_ref, gw_out, store_sem.at[1])
-    gw_store.start()
+    sum_store = pltpu.make_async_copy(totals, sum_out, store_sem.at[1])
+    sum_store.start()
 
     @pl.when(owns(me))
     def _():
@@ -422,26 +418,25 @@
             copy.wait_send()
 
     gf_store.wait()
+    sum_store.wait()
+
+
+def deliver(gf_in, sum_in, gf_out, gw_out, gf_ref, sum_ref, gw_ref, sem):
+    gf_load = pltpu.make_async_copy(gf_in, gf_ref, sem.at[0])
+    sum_load = pltpu.make_async_copy(sum_in, sum_ref, sem.at[1])
+    gf_store = pltpu.make_async_copy(gf_ref, gf_out, sem.at[2])
+    gw_store = pltpu.make_async_copy(gw_ref, gw_out, sem.at[3])
+    sum_load.start()
+    gf_load.start()
+    sum_load.wait()
+    whole = sum_ref[...].reshape(PARTS * PART_ROWS, 96)[0:144]
+    for a in range(3):
+        gw_ref[9 * a : 9 * (a + 1)] = whole[:, 32 * a : 32 * (a + 1)].reshape(9, 16, 32)
+    gw_store.start()
+    gf_load.wait()
+    gf_store.start()
     gw_store.wait()
-
-
-def deliver(gf_in, gw_in, gf_out, gw_out, gf_ref, gw_ref, sem):
-    steps = ((gf_in, gf_ref, gf_out), (gw_in, gw_ref, gw_out))
-    loads = [
-        pltpu.make_async_copy(source, held, sem.at[0, k])
-        for k, (source, held, _) in enumerate(steps)
-    ]
-    stores = [
-        pltpu.make_async_copy(held, target, sem.at[1, k])
-        for k, (_, held, target) in enumerate(steps)
-    ]
-    for load in loads:
-        load.start()
-    for load, store in zip(loads, stores):
-        load.wait()
-        store.start()
-    for store in stores:
-        store.wait()
+    gf_store.wait()
 
 
 def local(features, out_grad, weight, occupancy, neighbours):
@@ -460,12 +455,11 @@
 
     results = pl.pallas_call(
         body,
-        out_shape=outs,
+        out_shape=(outs[0], jax.ShapeDtypeStruct((PARTS,) + part, jnp.float32)),
         in_specs=[hbm] * 5,
         out_specs=(hbm, hbm),
         scratch_shapes=[
             pltpu.VMEM(features.shape, jnp.bfloat16),
-            pltpu.VMEM(weight.shape, jnp.float32),
             pltpu.SemaphoreType.DMA((2,)),
             pltpu.VMEM(features.shape, jnp.bfloat16),
             pltpu.VMEM(out_grad.shape, jnp.bfloat16),
@@ -501,8 +495,9 @@
         out_specs=(hbm, hbm),
         scratch_shapes=[
             pltpu.VMEM(features.shape, jnp.bfloat16),
+            pltpu.VMEM((PARTS,) + part, jnp.float32),
             pltpu.VMEM(weight.shape, jnp.float32),
-            pltpu.SemaphoreType.DMA((2, 2)),
+            pltpu.SemaphoreType.DMA((4,)),
         ],
         compiler_params=pltpu.CompilerParams(vmem_limit_bytes=limit),
         name="deliver",

time: 20.6 us -> 20.5 us (level)
  no operation moved by 1% of the time
where the time goes in v4:
time: 20.5 us; the launch traced here: 20.3 us
  Pallas kernels  19.7 us (96%)
  between operations  0.64 us (3%)
    pallas_call x1, Pallas kernels, local(): pl.pallas_call(body, out_shape=(outs[0], jax.ShapeDtypeStruct((PARTS,) +...  17.9 us
    pallas_call x1, Pallas kernels, local(): pl.pallas_call(deliver, out_shape=outs, in_specs=[hbm, hbm], out_specs=(h...  1.75 us

profile of v4, /device:TPU:0, one launch (start us, length us, event | category | flops | bytes accessed | tf_op | source)
XLA Modules:
  0.0 20.3 jit_solution(8399918463863044581)
XLA Ops:
  0.6 17.9 %brick_conv_backward.1 = (bf16[8,16,512]{2,1,0:T(8,128)(2,1)}, f32[4,40,96]{2,1,0:T(8,128)}) custom-call(bf16[8,16,512]{2,1,0:T(8,128)(2,1)} %refs_0_.1, bf16[8,16,512]{2,1,0:T(8,128)(2,1)} %refs_1_.1, bf16[27,16,32]{2,1,0:T(8,128)(2,1)} %refs_2_.1, s32[8,512]{1,0:T(8,128)} %refs_3_.1, s32[8,27]{1,0:T(8,128)} %refs_4_.1), custom_call_target="tpu_custom_call" | custom-call | tf_op jit(solution)/shard_map/brick_conv_backward/pallas_call | solution.py:456
  18.6 1.8 %deliver.1 = (bf16[8,16,512]{2,1,0:T(8,128)(2,1)}, f32[27,16,32]{2,1,0:T(8,128)}) custom-call(bf16[8,16,512]{2,1,0:T(8,128)(2,1)} %get-tuple-element.4.gf_in, f32[4,40,96]{2,1,0:T(8,128)} %get-tuple-element.5.sum_in), custom_call_target="tpu_custom_call" | custom-call | tf_op jit(solution)/shard_map/deliver/pallas_call | solution.py:491

commit v5 on v4

--- a/solution.py
+++ b/solution.py
@@ -133,24 +133,18 @@
         )
 
     below, above = me > 0, me < count - 1
-    plain = jnp.logical_not(owns(me))
-    meet_below = below & plain & jnp.logical_not(owns(me - 1))
-    meet_above = above & plain & jnp.logical_not(owns(me + 1))
-
     @pl.when(owns(me))
     def _():
         each_peer(lambda peer, j: greet(peer, chan))
 
-    @pl.when(plain)
-    def _():
-        for q in range(PARTS):
-            greet(first + q, chan)
-
-    @pl.when(meet_below)
+    tell_below = below & jnp.logical_not(owns(me))
+    tell_above = above & jnp.logical_not(owns(me))
+
+    @pl.when(tell_below)
     def _():
         greet(me - 1, chan)
 
-    @pl.when(meet_above)
+    @pl.when(tell_above)
     def _():
         greet(me + 1, chan)
 
@@ -217,8 +211,10 @@
     def _():
         grads[EDGE + 1] = zero_plane
 
-    met = jnp.where(plain, PARTS, count - 1) + 1
-    for more in (below, above, meet_below, meet_above):
+    met = jnp.where(owns(me), PARTS - 1, PARTS) + 1
+    hear_below = below & jnp.logical_not(owns(me - 1))
+    hear_above = above & jnp.logical_not(owns(me + 1))
+    for more in (below, above, hear_below, hear_above):
         met = met + more.astype(jnp.int32)
     pl.semaphore_wait(barrier, met)
 

time: 20.5 us -> 19.9 us (0.971)
  Pallas kernels: 19.7 us -> 19 us
    pallas_call x1, Pallas kernels: 17.9 us -> 17.3 us  [local(): pl.pallas_call(body, out_shape=(outs[0], jax.ShapeDtypeStruct((PARTS,) +...]
where the time goes in v5:
time: 19.9 us; the launch traced here: 19.7 us
  Pallas kernels  19 us (95%)
  between operations  0.64 us (3%)
    pallas_call x1, Pallas kernels, local(): pl.pallas_call(body, out_shape=(outs[0], jax.ShapeDtypeStruct((PARTS,) +...  17.3 us
    pallas_call x1, Pallas kernels, local(): pl.pallas_call(deliver, out_shape=outs, in_specs=[hbm, hbm], out_specs=(h...  1.75 us

profile of v5, /device:TPU:0, one launch (start us, length us, event | category | flops | bytes accessed | tf_op | source)
XLA Modules:
  0.0 19.7 jit_solution(7166305387185283174)
XLA Ops:
  0.6 17.3 %brick_conv_backward.1 = (bf16[8,16,512]{2,1,0:T(8,128)(2,1)}, f32[4,40,96]{2,1,0:T(8,128)}) custom-call(bf16[8,16,512]{2,1,0:T(8,128)(2,1)} %refs_0_.1, bf16[8,16,512]{2,1,0:T(8,128)(2,1)} %refs_1_.1, bf16[27,16,32]{2,1,0:T(8,128)(2,1)} %refs_2_.1, s32[8,512]{1,0:T(8,128)} %refs_3_.1, s32[8,27]{1,0:T(8,128)} %refs_4_.1), custom_call_target="tpu_custom_call" | custom-call | tf_op jit(solution)/shard_map/brick_conv_backward/pallas_call | solution.py:452
  17.9 1.8 %deliver.1 = (bf16[8,16,512]{2,1,0:T(8,128)(2,1)}, f32[27,16,32]{2,1,0:T(8,128)}) custom-call(bf16[8,16,512]{2,1,0:T(8,128)(2,1)} %get-tuple-element.4.gf_in, f32[4,40,96]{2,1,0:T(8,128)} %get-tuple-element.5.sum_in), custom_call_target="tpu_custom_call" | custom-call | tf_op jit(solution)/shard_map/deliver/pallas_call | solution.py:487
